TPU v7x, 128 devices: a whole 4x4x4 slice. The times are simulated.
128 devices in a mesh: sec: 2 (over core), dev: 64 (over y, x, z).
Axes of the slice: x: 4, y: 4, z: 4, core: 2. Of those that a mesh axis runs over, the one named last changes fastest.
Arguments:
- queries: bfloat16 [512, 128, 576], P(('sec', 'dev')), may hold values from -36 to 36
- latent_cache: bfloat16 [512, 2048, 576], P(('sec', 'dev')), may hold values from -6 to 6
- lengths: int32 [512], P(('sec', 'dev')), may hold values from 1 to 2048, 524288 in all
- rows_in: bfloat16 [4096, 3584], P(('sec', 'dev')), may hold values from -6 to 6
- routes: int32 [4096, 8], P(('sec', 'dev')), may hold values from 0 to 63, all different within a row; in each aligned block of 32 rows (0 to 31, 32 to 63, ...) at most 8 rows name the same one
- router_weight: bfloat16 [3584, 64], replicated, may hold values from -0.09375 to 0.09375
- gate_weight: bfloat16 [64, 3584, 1024], P('dev', None, 'sec'), may hold values from -0.09375 to 0.09375
- up_weight: bfloat16 [64, 3584, 1024], P('dev', None, 'sec'), may hold values from -0.09375 to 0.09375
- down_weight: bfloat16 [64, 1024, 3584], P('dev', 'sec'), may hold values from -0.1875 to 0.1875
Outputs:
- latent_out: bfloat16 [512, 128, 512], P(('sec', 'dev'))
- moe_out: bfloat16 [4096, 3584], P(('sec', 'dev'))
Inputs may be any that keep to these rules, and one draw needn't show every extreme that they name: `routes`: each row names 8 different experts; among the rows of one device no expert is named more than 8 times, a bound that some block reaches. `lengths`: the largest length is exactly 2048.
All inputs are finite; a program needn't handle non-finite values. No bound on the sum of `lengths` on one device may be relied on, other than what follows from the above.
Results may differ from a plain program's by a relative error of at most 0.012.
Values may be sent and summed in bfloat16 or wider, within the bound.
A program may use at most 128 MiB of HBM per device.

v0:
```python
import jax
import jax.numpy as jnp
from jax import lax
from jax.sharding import PartitionSpec as P

LATENT = 512


route_scale = 2.5
score_scale = 192.0 ** (-0.5)


def attend(queries, latent_cache, lengths):
    scores = (
        jnp.einsum("rhc,rlc->rhl", queries, latent_cache, preferred_element_type=jnp.float32)
        * score_scale
    )
    position = lax.broadcasted_iota(jnp.int32, (1, 1, latent_cache.shape[1]), 2)
    in_cache = position < lengths[:, None, None]
    scores = jnp.where(in_cache, scores, jnp.float32(-1e30))
    row_peak = jnp.max(scores, axis=2, keepdims=True)
    expo = jnp.exp(scores - row_peak)
    weights = (expo / jnp.sum(expo, axis=2, keepdims=True)).astype(jnp.bfloat16)
    values = latent_cache[:, :, :LATENT]
    return jnp.einsum("rhl,rlc->rhc", weights, values, preferred_element_type=jnp.float32).astype(
        jnp.bfloat16
    )


def dispatch(outgoing):
    return lax.all_to_all(outgoing, "dev", split_axis=0, concat_axis=0, tiled=True)


def halves_sum(flat_rows, gate_full, up_full, down_full, half_width):
    gate_part = jnp.dot(flat_rows, gate_full, preferred_element_type=jnp.float32)
    up_part = jnp.dot(flat_rows, up_full, preferred_element_type=jnp.float32)
    hidden = (jax.nn.silu(gate_part) * up_part).astype(jnp.bfloat16)
    first = jnp.dot(
        hidden[:, :half_width], down_full[:half_width], preferred_element_type=jnp.float32
    )
    second = jnp.dot(
        hidden[:, half_width:], down_full[half_width:], preferred_element_type=jnp.float32
    )
    first = lax.optimization_barrier(first.astype(jnp.bfloat16)).astype(jnp.float32)
    second = lax.optimization_barrier(second.astype(jnp.bfloat16)).astype(jnp.float32)
    return (first + second).astype(jnp.bfloat16)


def per_device(
    queries,
    latent_cache,
    lengths,
    rows_in,
    routes,
    router_weight,
    gate_weight,
    up_weight,
    down_weight,
):
    n_owners = lax.axis_size("dev")
    tok_rows, top_count = routes.shape
    width = rows_in.shape[1]
    experts_all = router_weight.shape[1]
    slots = max(2, 2 * tok_rows * top_count // n_owners)
    half_width = gate_weight.shape[2]
    logits = jnp.dot(rows_in, router_weight, preferred_element_type=jnp.float32)
    affinity = jax.nn.sigmoid(logits)
    expert_ids = lax.broadcasted_iota(jnp.int32, (1, 1, experts_all), 2)
    onehot = (routes[:, :, None] == expert_ids).astype(jnp.float32)
    chosen = jnp.sum(onehot * affinity[:, None, :], axis=2)
    gate_values = (route_scale * chosen / jnp.sum(chosen, axis=1, keepdims=True)).astype(
        jnp.bfloat16
    )
    flat_hot = onehot.reshape(tok_rows * top_count, experts_all)
    before = jnp.cumsum(flat_hot, axis=0) - flat_hot
    slot_index = jnp.sum(flat_hot * before, axis=1).astype(jnp.int32)
    target_slot = routes.reshape(-1) * slots + slot_index
    target = lax.broadcasted_iota(jnp.int32, (experts_all * slots, 1), 0)
    slot_map = (
        (target == target_slot[None, :])
        .astype(jnp.float32)
        .reshape(experts_all * slots, tok_rows, top_count)
    )
    row_map = jnp.sum(slot_map, axis=2).astype(jnp.bfloat16)
    outgoing = jnp.dot(row_map, rows_in, preferred_element_type=jnp.float32).astype(jnp.bfloat16)
    outgoing = outgoing.reshape(experts_all, slots, width)
    latent_out = attend(queries, latent_cache, lengths)
    received = dispatch(outgoing)
    gate_full, up_full, down_full = (
        lax.all_gather(gate_weight, "sec", axis=2, tiled=True),
        lax.all_gather(up_weight, "sec", axis=2, tiled=True),
        lax.all_gather(down_weight, "sec", axis=1, tiled=True),
    )
    flat_rows = received.reshape(-1, width)
    expert_rows = halves_sum(flat_rows, gate_full[0], up_full[0], down_full[0], half_width)
    expert_rows = expert_rows.reshape(n_owners, slots, width)
    returned = lax.all_to_all(expert_rows, "dev", split_axis=0, concat_axis=0, tiled=True)
    combine_map = jnp.sum(slot_map * gate_values.astype(jnp.float32)[None, :, :], axis=2).astype(
        jnp.bfloat16
    )
    moe_out = jnp.einsum(
        "sr,sd->rd",
        combine_map,
        returned.reshape(experts_all * slots, width),
        preferred_element_type=jnp.float32,
    )
    return (latent_out, moe_out.astype(jnp.bfloat16))


def solution(mesh):
    return jax.shard_map(
        per_device,
        mesh=mesh,
        in_specs=(
            P(("sec", "dev"), None, None),
            P(("sec", "dev"), None, None),
            P(("sec", "dev")),
            P(("sec", "dev"), None),
            P(("sec", "dev"), None),
            P(),
            P("dev", None, "sec"),
            P("dev", None, "sec"),
            P("dev", "sec", None),
        ),
        out_specs=(P(("sec", "dev"), None, None), P(("sec", "dev"), None)),
        check_vma=False,
    )
```

profile of v0, /device:TPU:0, one launch (start us, length us, event | category | flops | bytes accessed | tf_op | source)
XLA Modules:
  0.0 161.5 jit_solution(12911994994071089100)
XLA Ops:
  7.2 0.0 copy-start
  7.2 0.0 all-gather.6.cloned.1.call-start
  7.2 0.7 all-gather.6.cloned.1.call-update
  7.9 0.0 copy-start.4
  7.9 0.0 copy-start.2
  7.9 0.0 copy-start.3
  7.9 0.0 all-gather.4.cloned.1.call-start
  8.0 0.7 all-gather.4.cloned.1.call-update
  8.7 0.0 all-gather.8.cloned.1.call-start
  8.7 0.7 all-gather.8.cloned.1.call-update
  9.4 0.0 copy-done.4
  9.4 0.1 copy.27
  9.5 0.1 eq.51
  9.6 0.1 eq.47
  9.7 0.6 reduce-window.6
  10.3 0.2 slice_reduce_fusion
  10.5 0.1 fusion.31
  10.7 0.1 convert_element_type.77
  10.7 0.0 copy-done.2
  10.8 0.0 copy-done.3
  10.8 0.3 fusion.26
  11.0 0.5 select_reduce_fusion.1
  11.6 0.1 copy.32
  11.6 0.1 copy.33
  11.7 0.4 select_reduce_fusion
  12.1 1.1 fusion.7
  13.3 58.0 %all_to_all.10 = bf16[64,8,3584]{2,1,0:T(8,128)(2,1)} all-to-all(bf16[64,8,3584]{2,1,0:T(8,128)(2,1)S(1)} %fusion.7), channel_id=1, replica_groups=mesh['sec'=2,'dev'=64] {'dev'}, dimensions={0} | all-to-all | bytes 7340032 | tf_op jit(solution)/shard_map/all_to_all | solution.py:31
  71.3 0.0 all-gather.6.cloned.1.call-done
  71.3 11.3 %fusion.3 = f32[512,1024]{1,0:T(8,128)} fusion(bf16[1,3584,1024]{2,1,0:T(8,128)(2,1)} %all-gather.6.cloned.1.call-done, bf16[64,8,3584]{2,1,0:T(8,128)(2,1)} %all_to_all.10), kind=kOutput, calls=%fused_computation.3 | convolution fusion | flops 3758096384 | bytes 13107200 | tf_op jit(solution)/shard_map/dot_general | solution.py:36
  82.5 0.0 all-gather.4.cloned.1.call-done
  82.6 8.9 %multiply_convert_fusion = bf16[512,1024]{1,0:T(8,128)(2,1)S(1)} fusion(f32[512,1024]{1,0:T(8,128)} %fusion.3, bf16[1,3584,1024]{2,1,0:T(8,128)(2,1)} %all-gather.4.cloned.1.call-done, bf16[64,8,3584]{2,1,0:T(8,128)(2,1)} %all_to_all.10), kind=kOutput, calls=%fused_computation.23 | convolution fusion | flops 3761242112 | bytes 14155776 | tf_op jit(solution)/shard_map/dot_general | solution.py:35
  91.5 0.0 all-gather.8.cloned.1.call-done
  91.5 0.0 copy-start.6
  91.5 4.3 %convolution_convert_fusion.1 = bf16[512,3584]{1,0:T(8,128)(2,1)S(1)} fusion(bf16[1,1024,3584]{2,1,0:T(8,128)(2,1)} %all-gather.8.cloned.1.call-done, bf16[512,1024]{1,0:T(8,128)(2,1)S(1)} %multiply_convert_fusion), kind=kOutput, calls=%fused_computation.9 | convolution fusion | flops 1880883200 | bytes 7864320 | tf_op jit(solution)/shard_map/dot_general | solution.py:38
  95.8 0.0 copy-done.6
  95.8 2.1 %convolution_convert_fusion = bf16[512,3584]{1,0:T(8,128)(2,1)S(1)} fusion(bf16[1,1024,3584]{2,1,0:T(8,128)(2,1)S(1)} %copy-done.6, bf16[512,1024]{1,0:T(8,128)(2,1)S(1)} %multiply_convert_fusion), kind=kOutput, calls=%fused_computation.8 | convolution fusion | flops 1880883200 | bytes 7864320 | tf_op jit(solution)/shard_map/dot_general | solution.py:41
  97.9 2.8 %fusion.9 = bf16[64,8,3584]{2,1,0:T(8,128)(2,1)} fusion(bf16[512,3584]{1,0:T(8,128)(2,1)S(1)} %convolution_convert_fusion, bf16[512,3584]{1,0:T(8,128)(2,1)S(1)} %convolution_convert_fusion.1), kind=kLoop, calls=%fused_computation.17 | loop fusion | flops 7340032 | bytes 11010048 | tf_op jit(solution)/shard_map/reshape | solution.py:96
  100.7 0.0 copy-start.5
  100.7 6.0 %all-to-all-start.1 = ((bf16[64,8,3584]{2,1,0:T(8,128)(2,1)}), bf16[64,8,3584]{2,1,0:T(8,128)(2,1)}, u32[]{:S(2)}, u32[]{:S(2)}) async-start(bf16[64,8,3584]{2,1,0:T(8,128)(2,1)} %fusion.9), calls=%async_computation.1 | async-start | bytes 7340032 | tf_op jit(solution)/shard_map/all_to_all | solution.py:97
  106.7 0.0 copy-done.5
  106.7 0.1 iota_compare_fusion.4
  106.8 0.0 copy-done
  106.8 5.5 %fusion.44 = f32[4,128,2048]{2,1,0:T(8,128)S(1)} fusion(bf16[4,128,576]{1,2,0:T(8,128)(2,1)S(1)} %copy-done, bf16[4,2048,576]{1,2,0:T(8,128)(2,1)} %param.10), kind=kOutput, calls=%fused_computation.62 | convolution fusion | flops 1207959552 | bytes 14221312 | tf_op jit(solution)/shard_map/rhc,rlc->rhl/dot_general | solution.py:15
  112.3 0.0 copy-start.1
  112.3 1.9 %copy-done.1 = f32[4,128,2048]{2,1,0:T(8,128)} copy-done((f32[4,128,2048]{2,1,0:T(8,128)}, f32[4,128,2048]{2,1,0:T(8,128)S(1)}, u32[]{:S(2)}) %copy-start.1) | copy-done | bytes 4194328
  114.2 1.2 fusion.43
  115.5 8.6 %fusion.21 = bf16[4,128,512]{2,1,0:T(8,128)(2,1)} fusion(bf16[4,2048,576]{1,2,0:T(8,128)(2,1)} %param.10, f32[4,128]{1,0:T(4,128)S(1)} %fusion.43, f32[4,128,2048]{2,1,0:T(8,128)} %copy-done.1, pred[4,2048]{1,0:T(4,128)(4,1)S(1)} %iota_compare_fusion.4), kind=kOutput, calls=%fused_computation.28 | convolution fusion | flops 1079249408 | bytes 13117440 | tf_op jit(solution)/shard_map/rhl,rlc->rhc/dot_general | solution.py:25
  124.1 27.5 %all-to-all-done.1 = bf16[64,8,3584]{2,1,0:T(8,128)(2,1)} async-done(((bf16[64,8,3584]{2,1,0:T(8,128)(2,1)}), bf16[64,8,3584]{2,1,0:T(8,128)(2,1)}, u32[]{:S(2)}, u32[]{:S(2)}) %all-to-all-start.1) | async-done | bytes 3670048 | tf_op jit(solution)/shard_map/all_to_all | solution.py:97
  151.5 3.5 %convolution_convert_fusion.3 = bf16[32,3584]{1,0:T(8,128)(2,1)} fusion(bf16[64,8,3584]{2,1,0:T(8,128)(2,1)} %all-to-all-done.1, bf16[512,32]{0,1:T(8,128)(2,1)S(1)} %get-tuple-element.4), kind=kOutput, calls=%fused_computation.12 | convolution fusion | flops 117555200 | bytes 3932160 | tf_op jit(solution)/shard_map/sr,sd->rd/dot_general | solution.py:101
  (6 shorter events, 0.1 us)
Async XLA Ops:
  7.2 99.6 %copy-start = (bf16[4,128,576]{1,2,0:T(8,128)(2,1)S(1)}, bf16[4,128,576]{1,2,0:T(8,128)(2,1)}, u32[]{:S(2)}) copy-start(bf16[4,128,576]{1,2,0:T(8,128)(2,1)} %param.9) | copy-start | bytes 1769476
  7.2 64.1 %all-gather.6.cloned.1.call-start = ((), (), s32[]{:S(2)}) async-start(), calls=%async_computation.3 | async-start | bytes 11010048 | tf_op jit(solution)/shard_map/all_gather | solution.py:91
  7.9 1.5 copy-start.4
  7.9 2.8 %copy-start.2 = (bf16[32,3584]{1,0:T(8,128)(2,1)S(1)}, bf16[32,3584]{1,0:T(8,128)(2,1)}, u32[]{:S(2)}) copy-start(bf16[32,3584]{1,0:T(8,128)(2,1)} %param.12) | copy-start | bytes 688132
  7.9 2.8 %copy-start.3 = (bf16[3584,64]{0,1:T(8,128)(2,1)S(1)}, bf16[3584,64]{0,1:T(8,128)(2,1)}, u32[]{:S(2)}) copy-start(bf16[3584,64]{0,1:T(8,128)(2,1)} %param.14) | copy-start | bytes 1376260
  7.9 74.6 %all-gather.4.cloned.1.call-start = ((), (), s32[]{:S(2)}) async-start(), calls=%async_computation.2 | async-start | bytes 11010048 | tf_op jit(solution)/shard_map/all_gather | solution.py:90
  8.7 82.8 %all-gather.8.cloned.1.call-start = ((), (), s32[]{:S(2)}) async-start(), calls=%async_computation.4 | async-start | bytes 11010048 | tf_op jit(solution)/shard_map/all_gather | solution.py:92
  91.5 4.3 %copy-start.6 = (bf16[1,1024,3584]{2,1,0:T(8,128)(2,1)S(1)}, bf16[1,1024,3584]{2,1,0:T(8,128)(2,1)}, u32[]{:S(2)}) copy-start(bf16[1,1024,3584]{2,1,0:T(8,128)(2,1)} %all-gather.8.cloned.1.call-done) | copy-start | bytes 22020100
  100.7 6.0 %copy-start.5 = (s32[4]{0:T(128)S(1)}, s32[4]{0:T(128)}, u32[]{:S(2)}) copy-start(s32[4]{0:T(128)} %param.11) | copy-start | bytes 52
  100.7 50.8 %all-to-all-start.1 = ((bf16[64,8,3584]{2,1,0:T(8,128)(2,1)}), bf16[64,8,3584]{2,1,0:T(8,128)(2,1)}, u32[]{:S(2)}, u32[]{:S(2)}) async-start(bf16[64,8,3584]{2,1,0:T(8,128)(2,1)} %fusion.9), calls=%async_computation.1 | async-start | bytes 7340032 | tf_op jit(solution)/shard_map/all_to_all | solution.py:97
  112.3 1.9 %copy-start.1 = (f32[4,128,2048]{2,1,0:T(8,128)}, f32[4,128,2048]{2,1,0:T(8,128)S(1)}, u32[]{:S(2)}) copy-start(f32[4,128,2048]{2,1,0:T(8,128)S(1)} %fusion.44) | copy-start | bytes 12582916
Sparse Core Ops, SparseCore 0:
  9.7 23.4 all-gather.5
  34.8 22.3 all-gather.3
  58.8 22.3 all-gather.7
where the time goes:
time: 162 us
  blocking collectives  58 us (36%)
  matrix products  45.5 us (28%)
  waiting for transfers between devices  29.5 us (18%)
  between operations  13.9 us (9%)
  starting transfers between devices  6.09 us (4%)
  other arithmetic  5.85 us (4%)
  local copies, waits for them, and re-layouts  2.6 us (2%)
    all_to_all x1, blocking collectives, dispatch(): lax.all_to_all(outgoing, 'dev', split_axis=0, concat_axis=0, tiled=True)  58 us
    all_to_all x1, waiting for transfers between devices, per_device(): lax.all_to_all(expert_rows, 'dev', split_axis=0, concat_axis=0, tiled=True)  27.5 us
    dot_general x1, matrix products, halves_sum(): up_part = jnp.dot(flat_rows, up_full, preferred_element_type=jnp.float32)  11.3 us
    dot_general x1, matrix products, halves_sum(): jnp.dot(flat_rows, gate_full, preferred_element_type=jnp.float32)  8.92 us
    dot_general x1, matrix products, attend(): jnp.einsum('rhl,rlc->rhc', weights, values, preferred_element_type=jnp.fl...  8.58 us
    all_to_all x1, starting transfers between devices, per_device(): lax.all_to_all(expert_rows, 'dev', split_axis=0, concat_axis=0, tiled=True)  5.98 us
    dot_general x1, matrix products, attend(): jnp.einsum('rhc,rlc->rhl', queries, latent_cache, preferred_element_type=...  5.53 us
    dot_general x1, matrix products, halves_sum(): jnp.dot(hidden[:, :half_width], down_full[:half_width], preferred_element...  4.26 us
  transfers between devices with their start and end apart: 4, of which 1 were waited for; matrix products, arithmetic and copies ran while one was open for 24% of the time, Pallas kernels for 0%

commit v1 on v0

v1 whole, which is shorter than its diff:
```python
import jax
import jax.numpy as jnp
from jax import lax
from jax.experimental import pallas as pl
from jax.experimental.pallas import tpu as pltpu
from jax.sharding import PartitionSpec as P

MESH = pl.DeviceIdType.MESH
BF, F32 = jnp.bfloat16, jnp.float32
SIDE = 4
STRIDE = {"y": 16, "x": 4, "z": 1}
ROTATIONS = (("x", "y", "z"), ("z", "x", "y"), ("y", "z", "x"))
WIDTHS = (512, 512, 512, 768, 640, 640)
STARTS = tuple(sum(WIDTHS[:i]) for i in range(len(WIDTHS)))
FIRST, SECOND = (0, 1, 2), (3, 4, 5)
PARTS = FIRST + SECOND
EXTRA = 128
TOK, SLOTS, EXPERTS, LATENT = 32, 8, 64, 512
ROUTE_SCALE = 2.5
SCORE_SCALE = 192.0 ** (-0.5)
GATHER_A, GATHER_B, SPREAD, RETURN, SUM_B, SUM_A = range(6)


def block_map(r):
    a_axis, b_axis, c_axis = ROTATIONS[r]
    order = []
    for i in range(64):
        at = {c_axis: i // 16, b_axis: (i // 4) % 4, a_axis: i % 4}
        order.append(at["y"] * 16 + at["x"] * 4 + at["z"])
    return order


BLOCKS = tuple(block_map(r) for r in range(3))


def dot(a, b):
    return jnp.dot(a, b, preferred_element_type=F32)


def dot_nt(a, b):
    return lax.dot_general(a, b, (((1,), (1,)), ((), ())), preferred_element_type=F32)


def iota(shape, dim):
    return lax.broadcasted_iota(jnp.int32, shape, dim)


def body(len_ref, rows_ref, routes_ref, router_ref, q_hbm, kv_hbm, wg_hbm, wu_hbm, wd_hbm, lat_ref, out_ref, *scratch):
    scratch = list(scratch)

    def take(n):
        got = scratch[:n]
        del scratch[:n]
        return got

    wg, wu, wd, acc, qbuf, kvbuf, sbuf = take(7)
    hid, sel, comb = take(3), take(3), take(3)
    pb, tx, rx, back, r2, s2, r1 = (take(6) for _ in range(7))
    send_sem, recv_sem, w_local, w_send, w_recv, kv_sem, q_sem = take(7)

    sec, dev = lax.axis_index("sec"), lax.axis_index("dev")
    pos = {"y": lax.div(dev, 16), "x": lax.rem(lax.div(dev, 4), 4), "z": lax.rem(dev, 4)}

    def peer(axis, k):
        other = lax.rem(pos[axis] + k, SIDE)
        return (sec, dev + (other - pos[axis]) * STRIDE[axis])

    mate = (1 - sec, dev)

    barrier = pltpu.get_barrier_semaphore()
    for axis in ("x", "y", "z"):
        for k in (1, 2, 3):
            pl.semaphore_signal(barrier, inc=1, device_id=peer(axis, k), device_id_type=MESH)
    pl.semaphore_signal(barrier, inc=1, device_id=mate, device_id_type=MESH)

    def kv_copy(i):
        slot = lax.rem(i, 2)
        return pltpu.make_async_copy(kv_hbm.at[i], kvbuf.at[slot], kv_sem.at[slot])

    q_copy = pltpu.make_async_copy(q_hbm, qbuf, q_sem)
    q_copy.start()
    kv_copy(0).start()
    kv_copy(1).start()
    w_pairs = ((wg_hbm, wg), (wu_hbm, wu), (wd_hbm, wd))
    local = [pltpu.make_async_copy(src.at[0], dst.at[sec], w_local.at[i]) for i, (src, dst) in enumerate(w_pairs)]
    for copy in local:
        copy.start()

    affinity = jax.nn.sigmoid(dot(rows_ref[...], router_ref[...]))
    hot = jnp.zeros((TOK, EXPERTS), F32)
    expert = iota((TOK, EXPERTS), 1)
    for k in range(SLOTS):
        hot = hot + jnp.where(routes_ref[:, k : k + 1] == expert, 1.0, 0.0)
    chosen = hot * affinity
    gates = ROUTE_SCALE * chosen / jnp.sum(chosen, axis=1, keepdims=True)
    earlier = jnp.where(iota((TOK, TOK), 1) < iota((TOK, TOK), 0), 1.0, 0.0).astype(BF)
    place = hot * (dot(earlier, hot.astype(BF)) + 1.0)
    info = jnp.concatenate([place, gates], axis=1).astype(BF)

    def axes(p):
        return ROTATIONS[p % 3]

    for p in PARTS:
        a, b, _ = axes(p)
        mine = pb[p].at[pos[b], pos[a]]
        mine[:, : WIDTHS[p]] = rows_ref[:, STARTS[p] : STARTS[p] + WIDTHS[p]]
        if p in FIRST:
            mine[:, WIDTHS[p] :] = info

    def copies(phase, p):
        a, b, c = axes(p)
        made = []
        for k in (1, 2, 3):
            if phase == GATHER_A:
                axis, src = a, pb[p].at[pos[b], pos[a]]
                dst = src
            elif phase == GATHER_B:
                axis, src = b, pb[p].at[pos[b]]
                dst = src
            elif phase == SPREAD:
                axis, src, dst = c, tx[p].at[k - 1], rx[p].at[pos[c]]
            elif phase == RETURN:
                axis, src, dst = c, rx[p].at[lax.rem(pos[c] + k, SIDE)], back[p].at[3 - k]
            elif phase == SUM_B:
                axis, src, dst = b, pb[p].at[lax.rem(pos[b] + k, SIDE), :, :, pl.ds(0, WIDTHS[p])], r2[p].at[3 - k]
            else:
                axis, src, dst = a, s2[p].at[lax.rem(pos[a] + k, SIDE)], r1[p].at[3 - k]
            made.append(
                pltpu.make_async_remote_copy(
                    src_ref=src,
                    dst_ref=dst,
                    send_sem=send_sem.at[phase, p, k - 1],
                    recv_sem=recv_sem.at[phase, p, k - 1],
                    device_id=peer(axis, k),
                    device_id_type=MESH,
                )
            )
        return made

    flights = {}

    def send(phase, p):
        flights[phase, p] = copies(phase, p)
        for copy in flights[phase, p]:
            copy.start()

    def arrived(phase, p):
        for copy in flights[phase, p]:
            copy.wait_recv()

    def sent(phase, p):
        for copy in flights[phase, p]:
            copy.wait_send()

    pl.semaphore_wait(barrier, 10)
    for p in PARTS:
        send(GATHER_A, p)
    swaps = [
        pltpu.make_async_remote_copy(
            src_ref=src.at[0],
            dst_ref=dst.at[sec],
            send_sem=w_send.at[i],
            recv_sem=w_recv.at[i],
            device_id=mate,
            device_id_type=MESH,
        )
        for i, (src, dst) in enumerate(w_pairs)
    ]
    for copy in swaps:
        copy.start()

    def attend(i):
        kv_copy(i).wait()
        keys = kvbuf.at[lax.rem(i, 2)]
        query = qbuf[i]
        filled = len_ref[i]
        peak = jnp.full((128, 1), -1e30, F32)
        for j in range(4):
            s = dot_nt(query, keys[j * 512 : (j + 1) * 512]) * SCORE_SCALE
            s = jnp.where(iota((128, 512), 1) + j * 512 < filled, s, -1e30)
            sbuf[:, j * 512 : (j + 1) * 512] = s
            peak = jnp.maximum(peak, jnp.max(s, axis=1, keepdims=True))
        total = jnp.zeros((128, 1), F32)
        out = jnp.zeros((128, LATENT), F32)
        for j in range(4):
            e = jnp.exp(sbuf[:, j * 512 : (j + 1) * 512] - peak)
            total = total + jnp.sum(e, axis=1, keepdims=True)
            out = out + dot(e.astype(BF), keys[j * 512 : (j + 1) * 512, :LATENT])
        lat_ref[i] = (out / total).astype(BF)

    def lanes_of(r, shift):
        c = ROTATIONS[r][2]
        step = STRIDE[c]
        shape = (256, EXTRA)
        at = lax.rem(pos[c] + lax.div(iota(shape, 0), 64), SIDE)
        wanted = dev - pos[c] * step + at * step + shift
        return jnp.where(iota(shape, 1) == wanted, 1.0, 0.0).astype(BF)

    def info_of(r, half):
        w = WIDTHS[r]
        return pb[r][2 * half : 2 * half + 2, :, :, w : w + EXTRA].reshape(256, EXTRA)

    def build_sel(r):
        shape = (256, 256)
        row, col = iota(shape, 0), iota(shape, 1)
        same = lax.rem(lax.div(row, 8), 8) == lax.div(col, TOK)
        want = (lax.rem(row, 8) + 1).astype(F32)
        pick = lanes_of(r, 0)
        for half in range(2):
            got = dot_nt(pick, info_of(r, half))
            sel[r][half] = jnp.where(same & (got == want), 1.0, 0.0).astype(BF)

    def build_comb(r):
        shape = (256, 256)
        row, col = iota(shape, 0), iota(shape, 1)
        same = lax.rem(lax.div(col, 8), 8) == lax.div(row, TOK)
        want = (lax.rem(col, 8) + 1).astype(F32)
        pick, weigh = lanes_of(r, 0), lanes_of(r, EXPERTS)
        for half in range(2):
            got = dot_nt(info_of(r, half), pick)
            gate = dot_nt(info_of(r, half), weigh)
            comb[r][half] = jnp.where(same & (got == want), gate, 0.0).astype(BF)

    def spread(p):
        w, c = WIDTHS[p], axes(p)[2]
        for half in range(2):
            plane = pb[p][2 * half : 2 * half + 2, :, :, :w].reshape(256, w)
            got = dot(sel[p % 3][half], plane).astype(BF)
            at = slice(64 * half, 64 * half + 64)
            rx[p][pos[c], at] = got[:64]
            for j in range(1, SIDE):
                tx[p][j - 1, at] = got[64 * j : 64 * j + 64]

    def gate_up(p):
        w, r = WIDTHS[p], p % 3
        rows = slice(STARTS[p], STARTS[p] + w)

        @pl.loop(0, 2)
        def _(h):
            for g, weight in enumerate((wg, wu)):
                for n in range(2):
                    cols = slice(256 * n, 256 * n + 256)
                    got = dot(rx[p][...].reshape(512, w), weight[h, rows, cols])
                    for i in range(64):
                        piece = got[8 * i : 8 * i + 8]
                        if p == 0:
                            acc[h, g, BLOCKS[r][i], :, cols] = piece
                        else:
                            acc[h, g, BLOCKS[r][i], :, cols] += piece

    def hidden():
        @pl.loop(0, 2)
        def _(h):
            for n in range(4):
                cols = slice(128 * n, 128 * n + 128)
                pieces = []
                for i in range(64):
                    v = acc[h, 0, i, :, cols]
                    pieces.append(jax.nn.silu(v) * acc[h, 1, i, :, cols])
                for r in range(3):
                    for i in range(0, 64, 2):
                        pair = jnp.concatenate([pieces[BLOCKS[r][i]], pieces[BLOCKS[r][i + 1]]], axis=0)
                        hid[r][h, 8 * i : 8 * i + 16, cols] = pair.astype(BF)

    def down(p):
        w, r = WIDTHS[p], p % 3
        for n in range(0, w, 256):
            wide = min(256, w - n)
            cols = slice(STARTS[p] + n, STARTS[p] + n + wide)
            got = dot(hid[r][0], wd[0, :, cols]) + dot(hid[r][1], wd[1, :, cols])
            rx[p][:, :, n : n + wide] = got.astype(BF).reshape(SIDE, 128, wide)

    def combine(p):
        w, c = WIDTHS[p], axes(p)[2]
        for half in range(2):
            at = slice(64 * half, 64 * half + 64)
            got = jnp.concatenate([rx[p][pos[c], at]] + [back[p][j, at] for j in range(3)], axis=0)
            summed = dot(comb[p % 3][half], got).astype(BF)
            pb[p][2 * half : 2 * half + 2, :, :, :w] = summed.reshape(2, SIDE, TOK, w)

    def sum_b(p):
        w, b = WIDTHS[p], axes(p)[1]
        total = pb[p][pos[b], :, :, :w].astype(F32)
        for j in range(3):
            total = total + r2[p][j].astype(F32)
        s2[p][...] = total.astype(BF)

    def sum_a(p):
        a = axes(p)[0]
        total = s2[p][pos[a]].astype(F32)
        for j in range(3):
            total = total + r1[p][j].astype(F32)
        out_ref[:, STARTS[p] : STARTS[p] + WIDTHS[p]] = total.astype(BF)

    q_copy.wait()
    attend(0)
    kv_copy(2).start()
    for p in PARTS:
        arrived(GATHER_A, p)
        send(GATHER_B, p)
    attend(1)
    kv_copy(3).start()
    attend(2)
    for p in FIRST:
        arrived(GATHER_B, p)
        build_sel(p)
        spread(p)
        send(SPREAD, p)
    for r in range(3):
        build_comb(r)
    attend(3)
    for p in SECOND:
        arrived(GATHER_B, p)
        spread(p)
        send(SPREAD, p)
    for i in range(2):
        local[i].wait()
        swaps[i].wait_recv()
    for p in PARTS:
        arrived(SPREAD, p)
        gate_up(p)
    hidden()
    local[2].wait()
    swaps[2].wait_recv()
    for p in PARTS:
        down(p)
        send(RETURN, p)
    for p in PARTS:
        sent(GATHER_A, p)
        sent(GATHER_B, p)
        arrived(RETURN, p)
        combine(p)
        send(SUM_B, p)
    for p in PARTS:
        arrived(SUM_B, p)
        sum_b(p)
        send(SUM_A, p)
    for p in PARTS:
        arrived(SUM_A, p)
        sum_a(p)
    for copy in swaps:
        copy.wait_send()
    for phase in (SPREAD, RETURN, SUM_B, SUM_A):
        for p in PARTS:
            sent(phase, p)


def per_device(queries, latent_cache, lengths, rows_in, routes, router_weight, gate_weight, up_weight, down_weight):
    width = rows_in.shape[1]
    half = gate_weight.shape[2]
    vmem = pltpu.VMEM

    def each(make):
        return [make(p, WIDTHS[p]) for p in PARTS]

    scratch = [
        vmem((2, width, half), BF),
        vmem((2, width, half), BF),
        vmem((2, half, width), BF),
        vmem((2, 2, 64, 8, half), F32),
        vmem(queries.shape, BF),
        vmem((2,) + latent_cache.shape[1:], BF),
        vmem((queries.shape[1], latent_cache.shape[1]), F32),
    ]
    scratch += [vmem((2, 512, half), BF) for _ in range(3)]
    scratch += [vmem((2, 256, 256), BF) for _ in range(6)]
    scratch += each(lambda p, w: vmem((SIDE, SIDE, TOK, w + (EXTRA if p in FIRST else 0)), BF))
    scratch += each(lambda p, w: vmem((3, 128, w), BF))
    scratch += each(lambda p, w: vmem((SIDE, 128, w), BF))
    scratch += each(lambda p, w: vmem((3, 128, w), BF))
    scratch += each(lambda p, w: vmem((3, SIDE, TOK, w), BF))
    scratch += each(lambda p, w: vmem((SIDE, TOK, w), BF))
    scratch += each(lambda p, w: vmem((3, TOK, w), BF))
    dma = pltpu.SemaphoreType.DMA
    scratch += [dma((6, 6, 3)), dma((6, 6, 3)), dma((3,)), dma((3,)), dma((3,)), dma((2,)), dma]
    whole, stays = pl.BlockSpec(memory_space=pltpu.VMEM), pl.BlockSpec(memory_space=pl.ANY)
    return pl.pallas_call(
        body,
        out_shape=(
            jax.ShapeDtypeStruct(queries.shape[:2] + (LATENT,), BF),
            jax.ShapeDtypeStruct(rows_in.shape, BF),
        ),
        in_specs=[pl.BlockSpec(memory_space=pltpu.SMEM), whole, whole, whole] + [stays] * 5,
        out_specs=(whole, whole),
        scratch_shapes=scratch,
        compiler_params=pltpu.CompilerParams(
            collective_id=0, has_side_effects=True, vmem_limit_bytes=63 << 20
        ),
    )(lengths, rows_in, routes, router_weight, queries, latent_cache, gate_weight, up_weight, down_weight)


def solution(mesh):
    return jax.shard_map(
        per_device,
        mesh=mesh,
        in_specs=(
            P(("sec", "dev"), None, None),
            P(("sec", "dev"), None, None),
            P(("sec", "dev")),
            P(("sec", "dev"), None),
            P(("sec", "dev"), None),
            P(),
            P("dev", None, "sec"),
            P("dev", None, "sec"),
            P("dev", "sec", None),
        ),
        out_specs=(P(("sec", "dev"), None, None), P(("sec", "dev"), None)),
        check_vma=False,
    )
```

time: 162 us -> 113 us (0.70)
  Pallas kernels: 0 us -> 88.3 us
  blocking collectives: 58 us -> 0 us
  matrix products: 45.5 us -> 0 us
  waiting for transfers between devices: 29.5 us -> 0 us
  local copies, waits for them, and re-layouts: 2.6 us -> 23.4 us
  between operations: 13.9 us -> 0.64 us
  starting transfers between devices: 6.09 us -> 0 us
  other arithmetic: 5.85 us -> 0 us
    pallas_call x0 -> x1, Pallas kernels: none -> 88.3 us  [per_device(): pl.pallas_call(body, out_shape=(jax.ShapeDtypeStruct(queries.shape[:2] +...]
    all_to_all x1 -> x0, blocking collectives: 58 us -> none  [dispatch(): lax.all_to_all(outgoing, 'dev', split_axis=0, concat_axis=0, tiled=True)]
    dot_general x9 -> x0, matrix products: 45.5 us -> none  [the longest x1 11.3 us: halves_sum(): up_part = jnp.dot(flat_rows, up_full, preferred_element_type=jnp.float32)]
    all_to_all x1 -> x0, waiting for transfers between devices: 27.5 us -> none  [per_device(): lax.all_to_all(expert_rows, 'dev', split_axis=0, concat_axis=0, tiled=True)]
    unnamed x15 -> x6, local copies, waits for them, and re-layouts: 2.03 us -> 23.4 us
    all_to_all x1 -> x0, starting transfers between devices: 5.98 us -> none  [per_device(): lax.all_to_all(expert_rows, 'dev', split_axis=0, concat_axis=0, tiled=True)]
    reshape x1 -> x0, other arithmetic: 2.81 us -> none  [per_device(): expert_rows = expert_rows.reshape(n_owners, slots, width)]
    unnamed x3 -> x0, waiting for transfers between devices: 2.06 us -> none
  transfers between devices with their start and end apart: 4 -> 0, of which waited for: 1 -> 0; matrix products, arithmetic and copies ran while one was open for 24% -> 0% of each run, Pallas kernels for 0% -> 0%
where the time goes in v1:
time: 113 us; the launch traced here: 112 us
  Pallas kernels  88.3 us (78%)
  local copies, waits for them, and re-layouts  23.4 us (21%)
    pallas_call x1, Pallas kernels, per_device(): pl.pallas_call(body, out_shape=(jax.ShapeDtypeStruct(queries.shape[:2] +...  88.3 us
    unnamed x6, local copies, waits for them, and re-layouts  23.4 us

profile of v1, /device:TPU:0, one launch (start us, length us, event | category | flops | bytes accessed | tf_op | source)
XLA Modules:
  0.0 112.3 jit_solution(7815096464554705932)
XLA Ops:
  0.6 1.4 %copy.11.routes_ref = s32[32,8]{1,0:T(8,128)} copy(s32[32,8]{0,1:T(8,128)} %param.13) | data formatting | bytes 2048 | tf_op args[4]
  2.0 2.1 %copy.13.q_hbm = bf16[4,128,576]{2,1,0:T(8,128)(2,1)} copy(bf16[4,128,576]{1,2,0:T(8,128)(2,1)} %param.9) | data formatting | bytes 1179648 | tf_op args[0]
  4.1 2.2 %copy.12.router_ref = bf16[3584,64]{1,0:T(8,128)(2,1)} copy(bf16[3584,64]{0,1:T(8,128)(2,1)} %param.14) | data formatting | bytes 917504 | tf_op args[5]
  6.4 14.1 %copy.14.kv_hbm = bf16[4,2048,576]{2,1,0:T(8,128)(2,1)} copy(bf16[4,2048,576]{1,2,0:T(8,128)(2,1)} %param.10) | data formatting | bytes 18874368 | tf_op args[1]
  20.5 88.3 %shard_map.104 = (bf16[4,128,512]{2,1,0:T(8,128)(2,1)}, bf16[32,3584]{1,0:T(8,128)(2,1)}) custom-call(s32[4]{0:T(128)} %len_ref.1, bf16[32,3584]{1,0:T(8,128)(2,1)} %rows_ref.1, s32[32,8]{1,0:T(8,128)} %copy.11.routes_ref, bf16[3584,64]{1,0:T(8,128)(2,1)} %copy.12.router_ref, bf16[4,128,576]{2,1,0:T(8,128)(2,1)} %copy.13.q_hbm, ...), custom_call_target="tpu_custom_call" | custom-call | tf_op jit(solution)/shard_map/pallas_call | solution.py:377
  108.8 1.9 %copy.17 = bf16[4,128,512]{2,1,0:T(8,128)(2,1)} copy(bf16[4,128,512]{2,1,0:T(8,128)(2,1)} %get-tuple-element.4) | data formatting | bytes 1048576
  110.7 1.6 %copy.18 = bf16[32,3584]{1,0:T(8,128)(2,1)} copy(bf16[32,3584]{1,0:T(8,128)(2,1)} %get-tuple-element.5) | data formatting | bytes 458752

commit v2 on v1

--- a/solution.py
+++ b/solution.py
@@ -12,13 +12,14 @@
 ROTATIONS = (("x", "y", "z"), ("z", "x", "y"), ("y", "z", "x"))
 WIDTHS = (512, 512, 512, 768, 640, 640)
 STARTS = tuple(sum(WIDTHS[:i]) for i in range(len(WIDTHS)))
-FIRST, SECOND = (0, 1, 2), (3, 4, 5)
-PARTS = FIRST + SECOND
+PARTS = tuple(range(len(WIDTHS)))
+CHUNKS = tuple(PARTS[i : i + 3] for i in range(0, len(WIDTHS), 3))
+FIRST = CHUNKS[0]
 EXTRA = 128
 TOK, SLOTS, EXPERTS, LATENT = 32, 8, 64, 512
 ROUTE_SCALE = 2.5
 SCORE_SCALE = 192.0 ** (-0.5)
-GATHER_A, GATHER_B, SPREAD, RETURN, SUM_B, SUM_A = range(6)
+GATHER_A, GATHER_B, RELAY_B, SPREAD, RETURN, FAR_B, SUM_B, SUM_A = range(8)
 
 
 def block_map(r):
@@ -33,6 +34,13 @@
 BLOCKS = tuple(block_map(r) for r in range(3))
 
 
+PLACING = (
+    tuple(range(0, 64, 2)),
+    (),
+    tuple(y * 16 + x * 4 + z for x in range(4) for h in range(2) for y in (2 * h, 2 * h + 1) for z in (0, 2)),
+)
+
+
 def dot(a, b):
     return jnp.dot(a, b, preferred_element_type=F32)
 
@@ -53,10 +61,10 @@
         del scratch[:n]
         return got
 
-    wg, wu, wd, acc, qbuf, kvbuf, sbuf = take(7)
-    hid, sel, comb = take(3), take(3), take(3)
-    pb, tx, rx, back, r2, s2, r1 = (take(6) for _ in range(7))
-    send_sem, recv_sem, w_local, w_send, w_recv, kv_sem, q_sem = take(7)
+    wg, wu, wd, acc, qbuf, kvbuf, sbuf, gathered, hid = take(9)
+    sel, comb = take(3), take(3)
+    pb, tx, rx, back, far, r2, s2, r1 = (take(len(PARTS)) for _ in range(8))
+    send_sem, recv_sem, w_local, w_send, w_recv, kv_sem, q_sem, turn = take(8)
 
     sec, dev = lax.axis_index("sec"), lax.axis_index("dev")
     pos = {"y": lax.div(dev, 16), "x": lax.rem(lax.div(dev, 4), 4), "z": lax.rem(dev, 4)}
@@ -86,16 +94,16 @@
     for copy in local:
         copy.start()
 
-    affinity = jax.nn.sigmoid(dot(rows_ref[...], router_ref[...]))
-    hot = jnp.zeros((TOK, EXPERTS), F32)
-    expert = iota((TOK, EXPERTS), 1)
+    affinity = jax.nn.sigmoid(dot_nt(router_ref[...], rows_ref[...]))
+    hot = jnp.zeros((EXPERTS, TOK), F32)
+    expert = iota((EXPERTS, TOK), 0)
     for k in range(SLOTS):
-        hot = hot + jnp.where(routes_ref[:, k : k + 1] == expert, 1.0, 0.0)
+        hot = hot + jnp.where(routes_ref[k : k + 1, :] == expert, 1.0, 0.0)
     chosen = hot * affinity
-    gates = ROUTE_SCALE * chosen / jnp.sum(chosen, axis=1, keepdims=True)
-    earlier = jnp.where(iota((TOK, TOK), 1) < iota((TOK, TOK), 0), 1.0, 0.0).astype(BF)
-    place = hot * (dot(earlier, hot.astype(BF)) + 1.0)
-    info = jnp.concatenate([place, gates], axis=1).astype(BF)
+    gates = ROUTE_SCALE * chosen / jnp.sum(chosen, axis=0, keepdims=True)
+    earlier = jnp.where(iota((TOK, TOK), 0) < iota((TOK, TOK), 1), 1.0, 0.0).astype(BF)
+    place = hot * (dot(hot.astype(BF), earlier) + 1.0)
+    info = jnp.concatenate([place, gates], axis=0).T.astype(BF)
 
     def axes(p):
         return ROTATIONS[p % 3]
@@ -107,35 +115,47 @@
         if p in FIRST:
             mine[:, WIDTHS[p] :] = info
 
+    def near(axis, k):
+        return lax.rem(pos[axis] + k, SIDE)
+
     def copies(phase, p):
         a, b, c = axes(p)
-        made = []
-        for k in (1, 2, 3):
-            if phase == GATHER_A:
-                axis, src = a, pb[p].at[pos[b], pos[a]]
-                dst = src
-            elif phase == GATHER_B:
-                axis, src = b, pb[p].at[pos[b]]
-                dst = src
-            elif phase == SPREAD:
-                axis, src, dst = c, tx[p].at[k - 1], rx[p].at[pos[c]]
-            elif phase == RETURN:
-                axis, src, dst = c, rx[p].at[lax.rem(pos[c] + k, SIDE)], back[p].at[3 - k]
-            elif phase == SUM_B:
-                axis, src, dst = b, pb[p].at[lax.rem(pos[b] + k, SIDE), :, :, pl.ds(0, WIDTHS[p])], r2[p].at[3 - k]
-            else:
-                axis, src, dst = a, s2[p].at[lax.rem(pos[a] + k, SIDE)], r1[p].at[3 - k]
-            made.append(
-                pltpu.make_async_remote_copy(
-                    src_ref=src,
-                    dst_ref=dst,
-                    send_sem=send_sem.at[phase, p, k - 1],
-                    recv_sem=recv_sem.at[phase, p, k - 1],
-                    device_id=peer(axis, k),
-                    device_id_type=MESH,
-                )
+        first, second = pl.ds(0, 2), pl.ds(2, 2)
+        if phase == GATHER_A:
+            src = pb[p].at[pos[b], pos[a]]
+            plan = [(a, k, src, src) for k in (1, 2, 3)]
+        elif phase == GATHER_B:
+            src = pb[p].at[pos[b]]
+            plan = [(b, k, src, src) for k in (1, 3)]
+        elif phase == RELAY_B:
+            up, low = pb[p].at[near(b, 3), first], pb[p].at[near(b, 1), second]
+            plan = [(b, 1, up, up), (b, 3, low, low)]
+        elif phase == SPREAD:
+            plan = [(c, k, tx[p].at[k - 1], rx[p].at[pos[c]]) for k in (1, 2, 3)]
+        elif phase == RETURN:
+            plan = [(c, k, rx[p].at[near(c, k)], back[p].at[3 - k]) for k in (1, 2, 3)]
+        elif phase == FAR_B:
+            cols = pl.ds(0, WIDTHS[p])
+            plan = [
+                (b, 1, pb[p].at[near(b, 2), first, :, cols], far[p].at[0]),
+                (b, 3, pb[p].at[near(b, 2), second, :, cols], far[p].at[1]),
+            ]
+        elif phase == SUM_B:
+            cols = pl.ds(0, WIDTHS[p])
+            plan = [(b, k, pb[p].at[near(b, k), :, :, cols], r2[p].at[k // 2]) for k in (1, 3)]
+        else:
+            plan = [(a, k, s2[p].at[near(a, k)], r1[p].at[3 - k]) for k in (1, 2, 3)]
+        return [
+            pltpu.make_async_remote_copy(
+                src_ref=src,
+                dst_ref=dst,
+                send_sem=send_sem.at[phase, p, i],
+                recv_sem=recv_sem.at[phase, p, i],
+                device_id=peer(axis, k),
+                device_id_type=MESH,
             )
-        return made
+            for i, (axis, k, src, dst) in enumerate(plan)
+        ]
 
     flights = {}
 
@@ -172,11 +192,11 @@
     def attend(i):
         kv_copy(i).wait()
         keys = kvbuf.at[lax.rem(i, 2)]
-        query = qbuf[i]
+        query = qbuf[i].T
         filled = len_ref[i]
         peak = jnp.full((128, 1), -1e30, F32)
         for j in range(4):
-            s = dot_nt(query, keys[j * 512 : (j + 1) * 512]) * SCORE_SCALE
+            s = dot(query, keys[:, j * 512 : (j + 1) * 512]) * SCORE_SCALE
             s = jnp.where(iota((128, 512), 1) + j * 512 < filled, s, -1e30)
             sbuf[:, j * 512 : (j + 1) * 512] = s
             peak = jnp.maximum(peak, jnp.max(s, axis=1, keepdims=True))
@@ -185,7 +205,7 @@
         for j in range(4):
             e = jnp.exp(sbuf[:, j * 512 : (j + 1) * 512] - peak)
             total = total + jnp.sum(e, axis=1, keepdims=True)
-            out = out + dot(e.astype(BF), keys[j * 512 : (j + 1) * 512, :LATENT])
+            out = out + dot_nt(e.astype(BF), keys[:LATENT, j * 512 : (j + 1) * 512])
         lat_ref[i] = (out / total).astype(BF)
 
     def lanes_of(r, shift):
@@ -231,44 +251,60 @@
             for j in range(1, SIDE):
                 tx[p][j - 1, at] = got[64 * j : 64 * j + 64]
 
-    def gate_up(p):
+    def place_rows(p):
         w, r = WIDTHS[p], p % 3
-        rows = slice(STARTS[p], STARTS[p] + w)
+        cols = slice(STARTS[p], STARTS[p] + w)
+        if r == 1:
+            gathered[:, cols] = rx[p][...].reshape(512, w)
+            return
+        source = {BLOCKS[r][i]: i for i in range(64)}
+        loaded = {}
+
+        def piece(block):
+            i = source[block]
+            if i // 2 not in loaded:
+                at = 16 * ((i // 2) % 8)
+                loaded[i // 2] = rx[p][i // 16, at : at + 16].astype(F32)
+            return loaded[i // 2][8 * (i % 2) : 8 * (i % 2) + 8]
+
+        for block in PLACING[r]:
+            pair = jnp.concatenate([piece(block), piece(block + 1)], axis=0)
+            gathered[8 * block : 8 * block + 16, cols] = pair.astype(BF)
+
+    def gate_up(chunk):
+        begin = STARTS[CHUNKS[chunk][0]]
+        rows = slice(begin, begin + sum(WIDTHS[p] for p in CHUNKS[chunk]))
 
         @pl.loop(0, 2)
         def _(h):
-            for g, weight in enumerate((wg, wu)):
-                for n in range(2):
-                    cols = slice(256 * n, 256 * n + 256)
-                    got = dot(rx[p][...].reshape(512, w), weight[h, rows, cols])
-                    for i in range(64):
-                        piece = got[8 * i : 8 * i + 8]
-                        if p == 0:
-                            acc[h, g, BLOCKS[r][i], :, cols] = piece
-                        else:
-                            acc[h, g, BLOCKS[r][i], :, cols] += piece
-
-    def hidden():
-        @pl.loop(0, 2)
-        def _(h):
-            for n in range(4):
-                cols = slice(128 * n, 128 * n + 128)
-                pieces = []
-                for i in range(64):
-                    v = acc[h, 0, i, :, cols]
-                    pieces.append(jax.nn.silu(v) * acc[h, 1, i, :, cols])
-                for r in range(3):
-                    for i in range(0, 64, 2):
-                        pair = jnp.concatenate([pieces[BLOCKS[r][i]], pieces[BLOCKS[r][i + 1]]], axis=0)
-                        hid[r][h, 8 * i : 8 * i + 16, cols] = pair.astype(BF)
+            for n in range(2):
+                cols = slice(256 * n, 256 * n + 256)
+                parts = []
+                for g, weight in enumerate((wg, wu)):
+                    got = dot(gathered[:, rows], weight[h, rows, cols])
+                    if chunk == 0:
+                        acc[h, g, :, cols] = got
+                    elif chunk < len(CHUNKS) - 1:
+                        acc[h, g, :, cols] += got
+                    else:
+                        parts.append(got + acc[h, g, :, cols])
+                if chunk == len(CHUNKS) - 1:
+                    hid[h, :, cols] = (jax.nn.silu(parts[0]) * parts[1]).astype(BF)
 
     def down(p):
         w, r = WIDTHS[p], p % 3
         for n in range(0, w, 256):
             wide = min(256, w - n)
             cols = slice(STARTS[p] + n, STARTS[p] + n + wide)
-            got = dot(hid[r][0], wd[0, :, cols]) + dot(hid[r][1], wd[1, :, cols])
-            rx[p][:, :, n : n + wide] = got.astype(BF).reshape(SIDE, 128, wide)
+            got = dot(hid[0], wd[0, :, cols]) + dot(hid[1], wd[1, :, cols])
+            if r == 1:
+                rx[p][:, :, n : n + wide] = got.astype(BF).reshape(SIDE, 128, wide)
+                continue
+            for i in range(0, 64, 2):
+                one, two = BLOCKS[r][i], BLOCKS[r][i + 1]
+                pair = jnp.concatenate([got[8 * one : 8 * one + 8], got[8 * two : 8 * two + 8]], axis=0)
+                at = 8 * (i % 16)
+                rx[p][i // 16, at : at + 16, n : n + wide] = pair.astype(BF)
 
     def combine(p):
         w, c = WIDTHS[p], axes(p)[2]
@@ -278,10 +314,16 @@
             summed = dot(comb[p % 3][half], got).astype(BF)
             pb[p][2 * half : 2 * half + 2, :, :, :w] = summed.reshape(2, SIDE, TOK, w)
 
+    def fold(p):
+        w, b = WIDTHS[p], axes(p)[1]
+        for k, half in ((1, 0), (3, 1)):
+            at = (near(b, k), pl.ds(2 * half, 2), slice(None), pl.ds(0, w))
+            pb[p][at] = (pb[p][at].astype(F32) + far[p][half].astype(F32)).astype(BF)
+
     def sum_b(p):
         w, b = WIDTHS[p], axes(p)[1]
         total = pb[p][pos[b], :, :, :w].astype(F32)
-        for j in range(3):
+        for j in range(2):
             total = total + r2[p][j].astype(F32)
         s2[p][...] = total.astype(BF)
 
@@ -292,60 +334,112 @@
             total = total + r1[p][j].astype(F32)
         out_ref[:, STARTS[p] : STARTS[p] + WIDTHS[p]] = total.astype(BF)
 
+    def begin_b(chunk):
+        for p in CHUNKS[chunk]:
+            arrived(GATHER_A, p)
+            send(GATHER_B, p)
+
+    def relay_b(chunk):
+        for p in CHUNKS[chunk]:
+            arrived(GATHER_B, p)
+            send(RELAY_B, p)
+
+    def begin_spread(chunk):
+        for p in CHUNKS[chunk]:
+            arrived(RELAY_B, p)
+            if chunk == 0:
+                build_sel(p)
+            spread(p)
+            send(SPREAD, p)
+
+    def expert_in(chunk):
+        for p in CHUNKS[chunk]:
+            arrived(SPREAD, p)
+            place_rows(p)
+        gate_up(chunk)
+
+    def expert_out(chunk):
+        for p in CHUNKS[chunk]:
+            down(p)
+            send(RETURN, p)
+
+    def begin_sum(chunk):
+        for p in CHUNKS[chunk]:
+            for phase in (GATHER_A, GATHER_B, RELAY_B):
+                sent(phase, p)
+            arrived(RETURN, p)
+            combine(p)
+            send(FAR_B, p)
+
+    def fold_b(chunk):
+        for p in CHUNKS[chunk]:
+            arrived(FAR_B, p)
+            fold(p)
+            send(SUM_B, p)
+
+    def begin_a(chunk):
+        for p in CHUNKS[chunk]:
+            arrived(SUM_B, p)
+            sum_b(p)
+            send(SUM_A, p)
+
+    def finish(chunk):
+        for p in CHUNKS[chunk]:
+            arrived(SUM_A, p)
+            sum_a(p)
+
+    def give_turn():
+        @pl.when(sec == 0)
+        def _():
+            pl.semaphore_signal(turn, inc=1, device_id=mate, device_id_type=MESH)
+
+    def take_turn():
+        @pl.when(sec == 1)
+        def _():
+            pl.semaphore_wait(turn, 1)
+
     q_copy.wait()
     attend(0)
     kv_copy(2).start()
-    for p in PARTS:
-        arrived(GATHER_A, p)
-        send(GATHER_B, p)
+    begin_b(0)
     attend(1)
     kv_copy(3).start()
+    begin_b(1)
+    relay_b(0)
     attend(2)
-    for p in FIRST:
-        arrived(GATHER_B, p)
-        build_sel(p)
-        spread(p)
-        send(SPREAD, p)
+    relay_b(1)
+    begin_spread(0)
     for r in range(3):
         build_comb(r)
+    begin_spread(1)
     attend(3)
-    for p in SECOND:
-        arrived(GATHER_B, p)
-        spread(p)
-        send(SPREAD, p)
     for i in range(2):
         local[i].wait()
         swaps[i].wait_recv()
-    for p in PARTS:
-        arrived(SPREAD, p)
-        gate_up(p)
-    hidden()
+    expert_in(0)
+    expert_in(1)
     local[2].wait()
     swaps[2].wait_recv()
-    for p in PARTS:
-        down(p)
-        send(RETURN, p)
-    for p in PARTS:
-        sent(GATHER_A, p)
-        sent(GATHER_B, p)
-        arrived(RETURN, p)
-        combine(p)
-        send(SUM_B, p)
-    for p in PARTS:
-        arrived(SUM_B, p)
-        sum_b(p)
-        send(SUM_A, p)
-    for p in PARTS:
-        arrived(SUM_A, p)
-        sum_a(p)
+    expert_out(0)
+    expert_out(1)
+    begin_sum(0)
+    begin_sum(1)
+    fold_b(0)
+    fold_b(1)
+    begin_a(0)
+    begin_a(1)
+    finish(0)
+    finish(1)
     for copy in swaps:
         copy.wait_send()
-    for phase in (SPREAD, RETURN, SUM_B, SUM_A):
+    for phase in (SPREAD, RETURN, FAR_B, SUM_B, SUM_A):
         for p in PARTS:
             sent(phase, p)
 
 
 def per_device(queries, latent_cache, lengths, rows_in, routes, router_weight, gate_weight, up_weight, down_weight):
+    queries, latent_cache = jnp.swapaxes(queries, 1, 2), jnp.swapaxes(latent_cache, 1, 2)
+    routes, router_weight = routes.T, router_weight.T
     width = rows_in.shape[1]
     half = gate_weight.shape[2]
     vmem = pltpu.VMEM
@@ -357,27 +451,29 @@
         vmem((2, width, half), BF),
         vmem((2, width, half), BF),
         vmem((2, half, width), BF),
-        vmem((2, 2, 64, 8, half), F32),
+        vmem((2, 2, 512, half), F32),
         vmem(queries.shape, BF),
         vmem((2,) + latent_cache.shape[1:], BF),
-        vmem((queries.shape[1], latent_cache.shape[1]), F32),
+        vmem((queries.shape[2], latent_cache.shape[2]), F32),
     ]
-    scratch += [vmem((2, 512, half), BF) for _ in range(3)]
+    scratch += [vmem((512, width), BF), vmem((2, 512, half), BF)]
     scratch += [vmem((2, 256, 256), BF) for _ in range(6)]
     scratch += each(lambda p, w: vmem((SIDE, SIDE, TOK, w + (EXTRA if p in FIRST else 0)), BF))
     scratch += each(lambda p, w: vmem((3, 128, w), BF))
     scratch += each(lambda p, w: vmem((SIDE, 128, w), BF))
     scratch += each(lambda p, w: vmem((3, 128, w), BF))
-    scratch += each(lambda p, w: vmem((3, SIDE, TOK, w), BF))
+    scratch += each(lambda p, w: vmem((2, 2, TOK, w), BF))
+    scratch += each(lambda p, w: vmem((2, SIDE, TOK, w), BF))
     scratch += each(lambda p, w: vmem((SIDE, TOK, w), BF))
     scratch += each(lambda p, w: vmem((3, TOK, w), BF))
     dma = pltpu.SemaphoreType.DMA
-    scratch += [dma((6, 6, 3)), dma((6, 6, 3)), dma((3,)), dma((3,)), dma((3,)), dma((2,)), dma]
+    scratch += [dma((8, len(PARTS), 3)), dma((8, len(PARTS), 3)), dma((3,)), dma((3,)), dma((3,)), dma((2,)), dma]
+    scratch += [pltpu.SemaphoreType.REGULAR]
     whole, stays = pl.BlockSpec(memory_space=pltpu.VMEM), pl.BlockSpec(memory_space=pl.ANY)
     return pl.pallas_call(
         body,
         out_shape=(
-            jax.ShapeDtypeStruct(queries.shape[:2] + (LATENT,), BF),
+            jax.ShapeDtypeStruct((queries.shape[0], queries.shape[2], LATENT), BF),
             jax.ShapeDtypeStruct(rows_in.shape, BF),
         ),
         in_specs=[pl.BlockSpec(memory_space=pltpu.SMEM), whole, whole, whole] + [stays] * 5,

time: 113 us -> 84.9 us (0.75)
  local copies, waits for them, and re-layouts: 23.4 us -> 3.51 us
  Pallas kernels: 88.3 us -> 80.6 us
    unnamed x6 -> x2, local copies, waits for them, and re-layouts: 23.4 us -> 3.51 us
    pallas_call x1, Pallas kernels: 88.3 us -> 80.6 us  [per_device(): pl.pallas_call(body, out_shape=(jax.ShapeDtypeStruct((queries.shape[0], q...]
where the time goes in v2:
time: 84.9 us; the launch traced here: 84.7 us
  Pallas kernels  80.6 us (95%)
  local copies, waits for them, and re-layouts  3.51 us (4%)
    pallas_call x1, Pallas kernels, per_device(): pl.pallas_call(body, out_shape=(jax.ShapeDtypeStruct((queries.shape[0], q...  80.6 us
    unnamed x2, local copies, waits for them, and re-layouts  3.51 us

profile of v2, /device:TPU:0, one launch (start us, length us, event | category | flops | bytes accessed | tf_op | source)
XLA Modules:
  0.0 84.7 jit_solution(3356282071773353442)
XLA Ops:
  0.6 80.6 %shard_map.104 = (bf16[4,128,512]{2,1,0:T(8,128)(2,1)}, bf16[32,3584]{1,0:T(8,128)(2,1)}) custom-call(s32[4]{0:T(128)} %len_ref.1, bf16[32,3584]{1,0:T(8,128)(2,1)} %rows_ref.1, s32[8,32]{1,0:T(8,128)} %bitcast.7, bf16[64,3584]{1,0:T(8,128)(2,1)} %bitcast.6, bf16[4,576,128]{2,1,0:T(8,128)(2,1)} %bitcast.5, bf16[4,576,2048]{2,1,0:T(8,128)(2,1)} %bitcast.4, ...), custom_call_target="tpu_custom_call" | custom-call | tf_op jit(solution)/shard_map/pallas_call | solution.py:473
  81.2 1.9 %copy.13 = bf16[4,128,512]{2,1,0:T(8,128)(2,1)} copy(bf16[4,128,512]{2,1,0:T(8,128)(2,1)} %get-tuple-element.4) | data formatting | bytes 1048576
  83.1 1.6 %copy.14 = bf16[32,3584]{1,0:T(8,128)(2,1)} copy(bf16[32,3584]{1,0:T(8,128)(2,1)} %get-tuple-element.5) | data formatting | bytes 458752

commit v3 on v2

--- a/solution.py
+++ b/solution.py
@@ -10,7 +10,7 @@
 SIDE = 4
 STRIDE = {"y": 16, "x": 4, "z": 1}
 ROTATIONS = (("x", "y", "z"), ("z", "x", "y"), ("y", "z", "x"))
-WIDTHS = (512, 512, 512, 768, 640, 640)
+WIDTHS = (512, 512, 512, 512, 384, 384, 256, 256, 256)
 STARTS = tuple(sum(WIDTHS[:i]) for i in range(len(WIDTHS)))
 PARTS = tuple(range(len(WIDTHS)))
 CHUNKS = tuple(PARTS[i : i + 3] for i in range(0, len(WIDTHS), 3))
@@ -53,7 +53,7 @@
     return lax.broadcasted_iota(jnp.int32, shape, dim)
 
 
-def body(len_ref, rows_ref, routes_ref, router_ref, q_hbm, kv_hbm, wg_hbm, wu_hbm, wd_hbm, lat_ref, out_ref, *scratch):
+def body(len_ref, rows_hbm, routes_hbm, router_hbm, q_hbm, kv_hbm, wg_hbm, wu_hbm, wd_hbm, lat_ref, out_ref, *scratch):
     scratch = list(scratch)
 
     def take(n):
@@ -61,10 +61,11 @@
         del scratch[:n]
         return got
 
+    rows_ref, routes_ref, router_ref = take(3)
     wg, wu, wd, acc, qbuf, kvbuf, sbuf, gathered, hid = take(9)
     sel, comb = take(3), take(3)
     pb, tx, rx, back, far, r2, s2, r1 = (take(len(PARTS)) for _ in range(8))
-    send_sem, recv_sem, w_local, w_send, w_recv, kv_sem, q_sem, turn = take(8)
+    send_sem, recv_sem, w_local, w_send, w_recv, kv_sem, q_sem, in_sem, info_send, info_recv = take(10)
 
     sec, dev = lax.axis_index("sec"), lax.axis_index("dev")
     pos = {"y": lax.div(dev, 16), "x": lax.rem(lax.div(dev, 4), 4), "z": lax.rem(dev, 4)}
@@ -85,35 +86,20 @@
         slot = lax.rem(i, 2)
         return pltpu.make_async_copy(kv_hbm.at[i], kvbuf.at[slot], kv_sem.at[slot])
 
+    small = [
+        pltpu.make_async_copy(src, dst, in_sem.at[i])
+        for i, (src, dst) in enumerate(((rows_hbm, rows_ref), (router_hbm, router_ref), (routes_hbm, routes_ref)))
+    ]
+    for copy in small:
+        copy.start()
     q_copy = pltpu.make_async_copy(q_hbm, qbuf, q_sem)
     q_copy.start()
     kv_copy(0).start()
-    kv_copy(1).start()
     w_pairs = ((wg_hbm, wg), (wu_hbm, wu), (wd_hbm, wd))
     local = [pltpu.make_async_copy(src.at[0], dst.at[sec], w_local.at[i]) for i, (src, dst) in enumerate(w_pairs)]
-    for copy in local:
-        copy.start()
-
-    affinity = jax.nn.sigmoid(dot_nt(router_ref[...], rows_ref[...]))
-    hot = jnp.zeros((EXPERTS, TOK), F32)
-    expert = iota((EXPERTS, TOK), 0)
-    for k in range(SLOTS):
-        hot = hot + jnp.where(routes_ref[k : k + 1, :] == expert, 1.0, 0.0)
-    chosen = hot * affinity
-    gates = ROUTE_SCALE * chosen / jnp.sum(chosen, axis=0, keepdims=True)
-    earlier = jnp.where(iota((TOK, TOK), 0) < iota((TOK, TOK), 1), 1.0, 0.0).astype(BF)
-    place = hot * (dot(hot.astype(BF), earlier) + 1.0)
-    info = jnp.concatenate([place, gates], axis=0).T.astype(BF)
 
     def axes(p):
         return ROTATIONS[p % 3]
-
-    for p in PARTS:
-        a, b, _ = axes(p)
-        mine = pb[p].at[pos[b], pos[a]]
-        mine[:, : WIDTHS[p]] = rows_ref[:, STARTS[p] : STARTS[p] + WIDTHS[p]]
-        if p in FIRST:
-            mine[:, WIDTHS[p] :] = info
 
     def near(axis, k):
         return lax.rem(pos[axis] + k, SIDE)
@@ -122,8 +108,8 @@
         a, b, c = axes(p)
         first, second = pl.ds(0, 2), pl.ds(2, 2)
         if phase == GATHER_A:
-            src = pb[p].at[pos[b], pos[a]]
-            plan = [(a, k, src, src) for k in (1, 2, 3)]
+            src = pb[p].at[pos[b], pos[a], :, pl.ds(0, WIDTHS[p])]
+            plan = [(a, k, src, src) for k in (2, 1, 3)]
         elif phase == GATHER_B:
             src = pb[p].at[pos[b]]
             plan = [(b, k, src, src) for k in (1, 3)]
@@ -131,9 +117,9 @@
             up, low = pb[p].at[near(b, 3), first], pb[p].at[near(b, 1), second]
             plan = [(b, 1, up, up), (b, 3, low, low)]
         elif phase == SPREAD:
-            plan = [(c, k, tx[p].at[k - 1], rx[p].at[pos[c]]) for k in (1, 2, 3)]
+            plan = [(c, k, tx[p].at[k - 1], rx[p].at[pos[c]]) for k in (2, 1, 3)]
         elif phase == RETURN:
-            plan = [(c, k, rx[p].at[near(c, k)], back[p].at[3 - k]) for k in (1, 2, 3)]
+            plan = [(c, k, rx[p].at[near(c, k)], back[p].at[3 - k]) for k in (2, 1, 3)]
         elif phase == FAR_B:
             cols = pl.ds(0, WIDTHS[p])
             plan = [
@@ -144,7 +130,7 @@
             cols = pl.ds(0, WIDTHS[p])
             plan = [(b, k, pb[p].at[near(b, k), :, :, cols], r2[p].at[k // 2]) for k in (1, 3)]
         else:
-            plan = [(a, k, s2[p].at[near(a, k)], r1[p].at[3 - k]) for k in (1, 2, 3)]
+            plan = [(a, k, s2[p].at[near(a, k)], r1[p].at[3 - k]) for k in (2, 1, 3)]
         return [
             pltpu.make_async_remote_copy(
                 src_ref=src,
@@ -172,9 +158,50 @@
         for copy in flights[phase, p]:
             copy.wait_send()
 
+    small[0].wait()
+    for p in PARTS:
+        a, b, _ = axes(p)
+        pb[p][pos[b], pos[a], :, : WIDTHS[p]] = rows_ref[:, STARTS[p] : STARTS[p] + WIDTHS[p]]
     pl.semaphore_wait(barrier, 10)
-    for p in PARTS:
+    for p in FIRST:
         send(GATHER_A, p)
+    for copy in small[1:]:
+        copy.wait()
+
+    affinity = jax.nn.sigmoid(dot_nt(router_ref[...], rows_ref[...]))
+    hot = jnp.zeros((EXPERTS, TOK), F32)
+    expert = iota((EXPERTS, TOK), 0)
+    for k in range(SLOTS):
+        hot = hot + jnp.where(routes_ref[k : k + 1, :] == expert, 1.0, 0.0)
+    chosen = hot * affinity
+    gates = ROUTE_SCALE * chosen / jnp.sum(chosen, axis=0, keepdims=True)
+    earlier = jnp.where(iota((TOK, TOK), 0) < iota((TOK, TOK), 1), 1.0, 0.0).astype(BF)
+    place = hot * (dot(hot.astype(BF), earlier) + 1.0)
+    info = jnp.concatenate([place, gates], axis=0).T.astype(BF)
+
+    info_flights = []
+    for r in FIRST:
+        a, b, _ = axes(r)
+        mine = pb[r].at[pos[b], pos[a], :, pl.ds(WIDTHS[r], EXTRA)]
+        mine[...] = info
+        for k in (2, 1, 3):
+            info_flights.append(
+                pltpu.make_async_remote_copy(
+                    src_ref=mine,
+                    dst_ref=mine,
+                    send_sem=info_send.at[r, k - 1],
+                    recv_sem=info_recv.at[r, k - 1],
+                    device_id=peer(a, k),
+                    device_id_type=MESH,
+                )
+            )
+    for copy in info_flights:
+        copy.start()
+    for p in PARTS[3:]:
+        send(GATHER_A, p)
+    kv_copy(1).start()
+    for copy in local:
+        copy.start()
     swaps = [
         pltpu.make_async_remote_copy(
             src_ref=src.at[0],
@@ -188,6 +215,7 @@
     ]
     for copy in swaps:
         copy.start()
+
 
     def attend(i):
         kv_copy(i).wait()
@@ -337,6 +365,9 @@
     def begin_b(chunk):
         for p in CHUNKS[chunk]:
             arrived(GATHER_A, p)
+            if chunk == 0:
+                for copy in info_flights[3 * p : 3 * p + 3]:
+                    copy.wait_recv()
             send(GATHER_B, p)
 
     def relay_b(chunk):
@@ -367,6 +398,9 @@
         for p in CHUNKS[chunk]:
             for phase in (GATHER_A, GATHER_B, RELAY_B):
                 sent(phase, p)
+            if p in FIRST:
+                for copy in info_flights[3 * p : 3 * p + 3]:
+                    copy.wait_send()
             arrived(RETURN, p)
             combine(p)
             send(FAR_B, p)
@@ -387,54 +421,58 @@
         for p in CHUNKS[chunk]:
             arrived(SUM_A, p)
             sum_a(p)
-
-    def give_turn():
-        @pl.when(sec == 0)
-        def _():
-            pl.semaphore_signal(turn, inc=1, device_id=mate, device_id_type=MESH)
-
-    def take_turn():
-        @pl.when(sec == 1)
-        def _():
-            pl.semaphore_wait(turn, 1)
 
     q_copy.wait()
     attend(0)
     kv_copy(2).start()
     begin_b(0)
+    begin_b(1)
+    begin_b(2)
     attend(1)
     kv_copy(3).start()
-    begin_b(1)
+    attend(2)
     relay_b(0)
-    attend(2)
     relay_b(1)
+    relay_b(2)
+    attend(3)
     begin_spread(0)
+    begin_spread(1)
+    begin_spread(2)
     for r in range(3):
         build_comb(r)
-    begin_spread(1)
-    attend(3)
     for i in range(2):
         local[i].wait()
         swaps[i].wait_recv()
     expert_in(0)
     expert_in(1)
+    expert_in(2)
     local[2].wait()
     swaps[2].wait_recv()
     expert_out(0)
     expert_out(1)
+    expert_out(2)
     begin_sum(0)
     begin_sum(1)
+    begin_sum(2)
     fold_b(0)
     fold_b(1)
+    fold_b(2)
     begin_a(0)
     begin_a(1)
+    begin_a(2)
     finish(0)
     finish(1)
+    finish(2)
     for copy in swaps:
         copy.wait_send()
     for phase in (SPREAD, RETURN, FAR_B, SUM_B, SUM_A):
         for p in PARTS:
             sent(phase, p)
+
+
+def hand_over(lat_in, moe_in, lat_out, moe_out):
+    lat_out[...] = lat_in[...]
+    moe_out[...] = moe_in[...]
 
 
 def per_device(queries, latent_cache, lengths, rows_in, routes, router_weight, gate_weight, up_weight, down_weight):
@@ -448,6 +486,9 @@
         return [make(p, WIDTHS[p]) for p in PARTS]
 
     scratch = [
+        vmem(rows_in.shape, BF),
+        vmem(routes.shape, jnp.int32),
+        vmem(router_weight.shape, BF),
         vmem((2, width, half), BF),
         vmem((2, width, half), BF),
         vmem((2, half, width), BF),
@@ -468,21 +509,28 @@
     scratch += each(lambda p, w: vmem((3, TOK, w), BF))
     dma = pltpu.SemaphoreType.DMA
     scratch += [dma((8, len(PARTS), 3)), dma((8, len(PARTS), 3)), dma((3,)), dma((3,)), dma((3,)), dma((2,)), dma]
-    scratch += [pltpu.SemaphoreType.REGULAR]
+    scratch += [dma((3,)), dma((3, 3)), dma((3, 3))]
     whole, stays = pl.BlockSpec(memory_space=pltpu.VMEM), pl.BlockSpec(memory_space=pl.ANY)
-    return pl.pallas_call(
+    results = pl.pallas_call(
         body,
         out_shape=(
             jax.ShapeDtypeStruct((queries.shape[0], queries.shape[2], LATENT), BF),
             jax.ShapeDtypeStruct(rows_in.shape, BF),
         ),
-        in_specs=[pl.BlockSpec(memory_space=pltpu.SMEM), whole, whole, whole] + [stays] * 5,
+        in_specs=[pl.BlockSpec(memory_space=pltpu.SMEM)] + [stays] * 8,
         out_specs=(whole, whole),
         scratch_shapes=scratch,
         compiler_params=pltpu.CompilerParams(
             collective_id=0, has_side_effects=True, vmem_limit_bytes=63 << 20
         ),
     )(lengths, rows_in, routes, router_weight, queries, latent_cache, gate_weight, up_weight, down_weight)
+    return pl.pallas_call(
+        hand_over,
+        out_shape=[jax.ShapeDtypeStruct(x.shape, x.dtype) for x in results],
+        in_specs=[whole, whole],
+        out_specs=[whole, whole],
+        compiler_params=pltpu.CompilerParams(vmem_limit_bytes=63 << 20),
+    )(*results)
 
 
 def solution(mesh):

time: 84.9 us -> 79.3 us (0.934)
  local copies, waits for them, and re-layouts: 3.51 us -> 0 us
  Pallas kernels: 80.6 us -> 78.5 us
    pallas_call x1, Pallas kernels: 80.6 us -> 76.5 us  [per_device(): pl.pallas_call(body, out_shape=(jax.ShapeDtypeStruct((queries.shape[0], q...]
    unnamed x2 -> x0, local copies, waits for them, and re-layouts: 3.51 us -> none
    pallas_call x0 -> x1, Pallas kernels: none -> 1.99 us  [per_device(): pl.pallas_call(hand_over, out_shape=[jax.ShapeDtypeStruct(x.shape, x.dtyp...]
where the time goes in v3:
time: 79.3 us; the launch traced here: 79.1 us
  Pallas kernels  78.5 us (99%)
    pallas_call x1, Pallas kernels, per_device(): pl.pallas_call(body, out_shape=(jax.ShapeDtypeStruct((queries.shape[0], q...  76.5 us
    pallas_call x1, Pallas kernels, per_device(): pl.pallas_call(hand_over, out_shape=[jax.ShapeDtypeStruct(x.shape, x.dtyp...  1.99 us

profile of v3, /device:TPU:0, one launch (start us, length us, event | category | flops | bytes accessed | tf_op | source)
XLA Modules:
  0.0 79.1 jit_solution(4047986221371056962)
XLA Ops:
  0.6 76.5 %shard_map.104 = (bf16[4,128,512]{2,1,0:T(8,128)(2,1)}, bf16[32,3584]{1,0:T(8,128)(2,1)}) custom-call(s32[4]{0:T(128)} %len_ref.1, bf16[32,3584]{1,0:T(8,128)(2,1)} %rows_hbm.1, s32[8,32]{1,0:T(8,128)} %bitcast.7, bf16[64,3584]{1,0:T(8,128)(2,1)} %bitcast.6, bf16[4,576,128]{2,1,0:T(8,128)(2,1)} %bitcast.5, bf16[4,576,2048]{2,1,0:T(8,128)(2,1)} %bitcast.4, ...), custom_call_target="tpu_custom_call" | custom-call | tf_op jit(solution)/shard_map/pallas_call | solution.py:514
  77.1 2.0 %shard_map.105 = (bf16[4,128,512]{2,1,0:T(8,128)(2,1)}, bf16[32,3584]{1,0:T(8,128)(2,1)}) custom-call(bf16[4,128,512]{2,1,0:T(8,128)(2,1)} %get-tuple-element.4.lat_in, bf16[32,3584]{1,0:T(8,128)(2,1)} %get-tuple-element.5.moe_in), custom_call_target="tpu_custom_call" | custom-call | tf_op jit(solution)/shard_map/pallas_call | solution.py:527

commit v4 on v3

--- a/solution.py
+++ b/solution.py
@@ -213,8 +213,6 @@
         )
         for i, (src, dst) in enumerate(w_pairs)
     ]
-    for copy in swaps:
-        copy.start()
 
 
     def attend(i):
@@ -428,6 +426,8 @@
     begin_b(0)
     begin_b(1)
     begin_b(2)
+    for copy in swaps:
+        copy.start()
     attend(1)
     kv_copy(3).start()
     attend(2)

time: 79.3 us -> 79.3 us (level)
  no operation moved by 1% of the time
where the time goes in v4:
time: 79.3 us; the launch traced here: 79.1 us
  Pallas kernels  78.5 us (99%)
    pallas_call x1, Pallas kernels, per_device(): pl.pallas_call(body, out_shape=(jax.ShapeDtypeStruct((queries.shape[0], q...  76.5 us
    pallas_call x1, Pallas kernels, per_device(): pl.pallas_call(hand_over, out_shape=[jax.ShapeDtypeStruct(x.shape, x.dtyp...  1.99 us

profile of v4, /device:TPU:0, one launch (start us, length us, event | category | flops | bytes accessed | tf_op | source)
XLA Modules:
  0.0 79.1 jit_solution(7852579865065117761)
XLA Ops:
  0.6 76.5 %shard_map.104 = (bf16[4,128,512]{2,1,0:T(8,128)(2,1)}, bf16[32,3584]{1,0:T(8,128)(2,1)}) custom-call(s32[4]{0:T(128)} %len_ref.1, bf16[32,3584]{1,0:T(8,128)(2,1)} %rows_hbm.1, s32[8,32]{1,0:T(8,128)} %bitcast.7, bf16[64,3584]{1,0:T(8,128)(2,1)} %bitcast.6, bf16[4,576,128]{2,1,0:T(8,128)(2,1)} %bitcast.5, bf16[4,576,2048]{2,1,0:T(8,128)(2,1)} %bitcast.4, ...), custom_call_target="tpu_custom_call" | custom-call | tf_op jit(solution)/shard_map/pallas_call | solution.py:514
  77.1 2.0 %shard_map.105 = (bf16[4,128,512]{2,1,0:T(8,128)(2,1)}, bf16[32,3584]{1,0:T(8,128)(2,1)}) custom-call(bf16[4,128,512]{2,1,0:T(8,128)(2,1)} %get-tuple-element.4.lat_in, bf16[32,3584]{1,0:T(8,128)(2,1)} %get-tuple-element.5.moe_in), custom_call_target="tpu_custom_call" | custom-call | tf_op jit(solution)/shard_map/pallas_call | solution.py:527
